TPU v7x, 512 devices: a whole 4x4x16 slice. The times are simulated.
512 devices in a mesh: chan: 32 (over z, y_lo), row: 2 (over core), col: 8 (over x, y_hi).
Axes of the slice: x: 4, y: 4 (y_hi: 2, y_lo: 2; y = y_hi * 2 + y_lo), z: 16, core: 2. Of those that a mesh axis runs over, the one named last changes fastest.
Arguments:
- volts: bfloat16 [2, 1024, 2, 52736], P(None, ('chan', 'row', 'col')), may hold values from -6 to 6
- taps: float32 [8, 512], replicated, may hold values from -2 to 2
- owner_map: int32 [384], replicated, may hold values from 0 to 255, as said below
- assign: int32 [512], replicated, may hold values from 0 to 511, each once
Outputs:
- visibility: bfloat16 [512, 2, 1024, 1024], P(('chan', 'col'), None, 'row')
Inputs may be any that keep to these rules, and one draw needn't show every extreme that they name: `owner_map`: each owner holds 1 to 2 channels, and some owner holds exactly 2. `assign`: A permutation of the stations.
All inputs are finite; a program needn't handle non-finite values.
Results may differ from a plain program's by a relative error of at most 0.0055.
Values may be sent and summed in bfloat16 or wider, within the bound.
A program may use at most 64 MiB of HBM per device.

v0:
```python
import math
import jax
import jax.numpy as jnp
from jax import lax
from jax.sharding import PartitionSpec as P

STATIONS = 512
NFFT = 512
TAPS = 8
BATCHES = 2
CAP = 2


def slot_table(owner_map, owner_count, slot_count):
    channel_count = owner_map.shape[0]
    ranking = jnp.argsort(owner_map * channel_count + jnp.arange(channel_count, dtype=jnp.int32))
    counts = jnp.sum(
        (owner_map[None, :] == jnp.arange(owner_count, dtype=jnp.int32)[:, None]).astype(jnp.int32),
        axis=1,
    )
    starts = jnp.cumsum(counts) - counts
    slot_index = jnp.arange(slot_count, dtype=jnp.int32)
    position = jnp.clip(starts[:, None] + slot_index[None, :], 0, channel_count - 1)
    channel = jnp.take(ranking, position, axis=0)
    is_live = slot_index[None, :] < counts[:, None]
    return (channel, is_live)


def shards(volts, taps, owner_map, assign):
    chan_count = lax.axis_size("chan")
    rows_count = lax.axis_size("row")
    cols_count = lax.axis_size("col")
    owner_count = chan_count * cols_count
    local_inputs = volts.shape[1]
    spec_len = volts.shape[3] // NFFT - TAPS + 1
    channel, is_live = slot_table(owner_map, owner_count, CAP)
    points = jnp.arange(NFFT, dtype=jnp.int32)
    phase = (points[:, None, None] * channel.T[None, :, :] % NFFT).astype(jnp.float32) * (
        2.0 * math.pi / NFFT
    )
    weight_live = is_live.T[None, :, :].astype(jnp.float32) / math.sqrt(NFFT)
    cosine = jnp.cos(phase) * weight_live
    sine = jnp.sin(phase) * weight_live
    table = jnp.stack(
        [jnp.stack([cosine, -sine], axis=1), jnp.stack([sine, cosine], axis=1)], axis=0
    )
    total_inputs = 2 * STATIONS
    positions = jnp.arange(total_inputs, dtype=jnp.int32)
    pick = 2 * jnp.take(assign, positions // 2, axis=0) + positions % 2
    device_of = pick // local_inputs
    within = pick % local_inputs
    chan_of = device_of // (rows_count * cols_count)
    row_of = device_of // cols_count % rows_count
    col_of = device_of % cols_count
    located = ((row_of * cols_count + col_of) * chan_count + chan_of) * local_inputs + within
    row_count = total_inputs // rows_count
    row_pick = lax.dynamic_slice_in_dim(located, lax.axis_index("row") * row_count, row_count)
    total = jnp.zeros((CAP, 2 * row_count, total_inputs), jnp.float32)
    for batch in range(BATCHES):
        signal = (
            volts[batch].astype(jnp.float32).reshape(local_inputs, 2, spec_len + TAPS - 1, NFFT)
        )
        summed = jnp.zeros((local_inputs, 2, spec_len, NFFT), jnp.float32)
        for tap_index in range(TAPS):
            summed = (
                summed
                + taps[tap_index][None, None, None, :]
                * signal[:, :, tap_index : tap_index + spec_len, :]
            )
        result = jnp.einsum("iasj,ajbkg->kgibs", summed, table, precision=lax.Precision.HIGHEST)
        turned = lax.all_to_all(
            lax.all_to_all(
                result.reshape(CAP, chan_count, cols_count, local_inputs, 2 * spec_len).astype(
                    jnp.bfloat16
                ),
                "chan",
                split_axis=1,
                concat_axis=3,
                tiled=True,
            ),
            "col",
            split_axis=2,
            concat_axis=3,
            tiled=True,
        )
        gathered = lax.all_gather(turned, "row", axis=3, tiled=True)
        flat = gathered.reshape(CAP, total_inputs, -1)
        width = flat.shape[2]
        rows = jnp.take(flat, row_pick, axis=1)
        split_rows = rows.reshape(CAP, row_count, width // (2 * spec_len), 2, spec_len)
        flipped = jnp.stack(
            [split_rows[:, :, :, 1, :], -split_rows[:, :, :, 0, :]], axis=3
        ).reshape(CAP, row_count, width)
        stacked = jnp.concatenate([rows, flipped], axis=1)
        columns = jnp.take(flat, located, axis=1)
        total = total + jnp.einsum(
            "kpx,kqx->kpq", stacked, columns, preferred_element_type=jnp.float32
        )
    scale = 1.0 / math.sqrt(2 * BATCHES * spec_len)
    return (total * scale).reshape(CAP, 2, row_count, total_inputs).astype(jnp.bfloat16)


def solution(mesh):
    placed = (P(None, ("chan", "row", "col"), None, None), P(), P(), P())
    return jax.shard_map(
        shards,
        mesh=mesh,
        in_specs=placed,
        out_specs=P(("chan", "col"), None, "row", None),
        check_vma=False,
    )
```

profile of v0, /device:TPU:1, one launch (start us, length us, event | category | flops | bytes accessed | tf_op | source)
XLA Modules:
  0.0 180.4 jit_solution(5233471085927798527)
XLA Ops:
  2.1 1.0 fusion.107
  3.4 3.8 %sort.17 = (s32[384]{0:T(512)}, s32[384]{0:T(512)S(1)}) sort(s32[384]{0:T(512)S(1)} %iota_add_fusion, s32[384]{0:T(512)S(1)} %iota.40), dimensions={0}, to_apply=%region_3.4 | sort | flops 3456 | bytes 6144 | tf_op jit(solution)/shard_map/jit(argsort)/sort | solution.py:16
  7.2 3.5 %gather_fusion = s32[512]{0:T(512)S(1)} fusion(s32[384]{0:T(512)S(1)} %get-tuple-element.8, s32[1024]{0:T(1024)S(1)} %pad_clamp_fusion.1), kind=kCustom, calls=%fused_computation.4 | custom fusion | bytes 6144 | tf_op jit(solution)/shard_map/jit(_take)/gather | solution.py:24
  11.7 1.5 reshape.293
  13.2 4.2 %fusion.71 = (f32[512,1,2,256]{3,0,2,1:T(8,128)S(1)}, f32[512,1,2,256]{3,0,2,1:T(8,128)S(1)}, f32[512,1,2,256]{3,0,2,1:T(8,128)S(1)}) fusion(f32[2,256]{1,0:T(2,128)S(1)} %compare_select_fusion.6, s32[2,256]{1,0:T(2,128)S(1)} %copy.54), kind=kLoop, calls=%fused_computation.100 | loop fusion | flops 4456448 | bytes 3149824 | tf_op jit(solution)/shard_map/neg | solution.py:45
  17.7 1.3 copy-done.1
  19.0 4.6 %fusion.6 = bf16[2,256,2,2,96]{1,4,2,0,3:T(8,128)(2,1)} fusion(f32[1,512,2,2,256]{4,1,0,3,2:T(8,128)S(1)} %get-tuple-element.14, f32[1,512,2,2,256]{4,1,0,3,2:T(8,128)S(1)} %get-tuple-element.13, f32[2,2,103,512]{3,2,1,0:T(8,128)S(1)} %copy-done.2, f32[512]{0:T(512)S(1)} %bitcast.127, f32[512]{0:T(512)S(1)} %bitcast.129, f32[512]{0:T(512)S(1)} %bitcast.117, ...), kind=kOutput, calls=%fused_computation.21 | convolution fusion | flops 2420113408 | bytes 10895360 | tf_op jit(solution)/shard_map/iasj,ajbkg->kgibs/dot_general | solution.py:70
  23.7 1.3 copy.56
  25.0 1.1 convert_element_type.68
  26.1 1.9 %copy.57 = bf16[2,32,8,2,192]{4,2,3,0,1:T(8,128)(2,1)} copy(bf16[2,32,8,2,192]{4,2,1,3,0:T(8,128)(2,1)} %convert_element_type.68) | data formatting | bytes 786432 | tf_op jit(solution)/shard_map/convert_element_type | solution.py:73
  28.0 17.0 %all-to-all-start = ((bf16[2,32,8,2,192]{4,2,3,0,1:T(8,128)(2,1)}), bf16[2,32,8,2,192]{4,2,3,0,1:T(8,128)(2,1)S(1)}, u32[]{:S(2)}, u32[]{:S(2)}) async-start(bf16[2,32,8,2,192]{4,2,3,0,1:T(8,128)(2,1)} %copy.57), calls=%async_computation | async-start | bytes 1048576 | tf_op jit(solution)/shard_map/all_to_all | solution.py:72
  45.1 1.5 reshape.294
  46.6 9.2 %fusion.7 = bf16[2,256,2,2,96]{1,4,2,0,3:T(8,128)(2,1)} fusion(f32[1,512,2,2,256]{4,1,0,3,2:T(8,128)} %copy-done.1, f32[1,512,2,2,256]{4,1,0,3,2:T(8,128)S(1)} %get-tuple-element.13, f32[2,2,103,512]{3,2,1,0:T(8,128)} %reshape.294, f32[512]{0:T(512)S(1)} %bitcast.128, f32[512]{0:T(512)S(1)} %bitcast.130, f32[512]{0:T(512)S(1)} %bitcast.118, ...), kind=kOutput, calls=%fused_computation.22 | convolution fusion | flops 2420113408 | bytes 10895360 | tf_op jit(solution)/shard_map/iasj,ajbkg->kgibs/dot_general | solution.py:70
  55.8 1.3 copy.65
  58.3 17.8 %all-to-all-done = bf16[2,32,8,2,192]{4,2,3,0,1:T(8,128)(2,1)S(1)} async-done(((bf16[2,32,8,2,192]{4,2,3,0,1:T(8,128)(2,1)}), bf16[2,32,8,2,192]{4,2,3,0,1:T(8,128)(2,1)S(1)}, u32[]{:S(2)}, u32[]{:S(2)}) %all-to-all-start) | async-done | bytes 393248 | tf_op jit(solution)/shard_map/all_to_all | solution.py:72
  76.0 5.2 %all-to-all-start.2 = ((bf16[2,32,8,2,192]{4,2,3,0,1:T(8,128)(2,1)}), bf16[2,32,8,2,192]{4,2,3,0,1:T(8,128)(2,1)S(1)}, u32[]{:S(2)}, u32[]{:S(2)}) async-start(bf16[2,32,8,2,192]{4,2,3,0,1:T(8,128)(2,1)} %copy.66), calls=%async_computation.2 | async-start | bytes 1048576 | tf_op jit(solution)/shard_map/all_to_all | solution.py:72
  82.3 29.5 %all-to-all-done.2 = bf16[2,32,8,2,192]{4,2,3,0,1:T(8,128)(2,1)S(1)} async-done(((bf16[2,32,8,2,192]{4,2,3,0,1:T(8,128)(2,1)}), bf16[2,32,8,2,192]{4,2,3,0,1:T(8,128)(2,1)S(1)}, u32[]{:S(2)}, u32[]{:S(2)}) %all-to-all-start.2) | async-done | bytes 393248 | tf_op jit(solution)/shard_map/all_to_all | solution.py:72
  111.7 6.3 %all-to-all-start.1 = ((bf16[2,1,8,64,192]{4,3,0,1,2:T(8,128)(2,1)}), bf16[2,1,8,64,192]{4,3,0,1,2:T(8,128)(2,1)S(1)}, u32[]{:S(2)}, u32[]{:S(2)}) async-start(bf16[2,1,8,64,192]{4,3,0,1,2:T(8,128)(2,1)} %copy.59), calls=%async_computation.1 | async-start | bytes 1048576 | tf_op jit(solution)/shard_map/all_to_all | solution.py:71
  118.1 6.9 %gather_fusion.1 = s32[1024]{0:T(1024)S(1)} fusion(s32[512]{0:T(512)S(1)} %copy-done, s32[1024]{0:T(1024)S(1)} %broadcast_clamp_fusion), kind=kCustom, calls=%fused_computation.5 | custom fusion | bytes 12288 | tf_op jit(solution)/shard_map/jit(_take)/gather | solution.py:49
  126.6 6.0 %all-to-all-start.3 = ((bf16[2,1,8,64,192]{4,3,0,1,2:T(8,128)(2,1)}), bf16[2,1,8,64,192]{4,3,0,1,2:T(8,128)(2,1)S(1)}, u32[]{:S(2)}, u32[]{:S(2)}) async-start(bf16[2,1,8,64,192]{4,3,0,1,2:T(8,128)(2,1)} %copy.68), calls=%async_computation.3 | async-start | bytes 1048576 | tf_op jit(solution)/shard_map/all_to_all | solution.py:71
  132.9 8.2 %all-to-all-done.3 = bf16[2,1,8,64,192]{4,3,0,1,2:T(8,128)(2,1)S(1)} async-done(((bf16[2,1,8,64,192]{4,3,0,1,2:T(8,128)(2,1)}), bf16[2,1,8,64,192]{4,3,0,1,2:T(8,128)(2,1)S(1)}, u32[]{:S(2)}, u32[]{:S(2)}) %all-to-all-start.3) | async-done | bytes 393248 | tf_op jit(solution)/shard_map/all_to_all | solution.py:71
  141.4 7.5 %all_gather.7 = bf16[2,1,1,1024,192]{3,4,2,1,0:T(8,128)(2,1)S(1)} all-gather(bf16[2,1,1,512,192]{3,4,2,1,0:T(8,128)(2,1)S(1)} %copy.70), channel_id=1, replica_groups=mesh['chan'=32,'row'=2,'col'=8] {'row'}, dimensions={3}, use_global_device_ids=true | all-gather | bytes 1179648 | tf_op jit(solution)/shard_map/all_gather | solution.py:86
  149.8 2.6 %all_gather.6 = bf16[2,1,1,1024,192]{3,4,2,1,0:T(8,128)(2,1)S(1)} all-gather(bf16[2,1,1,512,192]{3,4,2,1,0:T(8,128)(2,1)S(1)} %copy.61), channel_id=1, replica_groups=mesh['chan'=32,'row'=2,'col'=8] {'row'}, dimensions={3}, use_global_device_ids=true | all-gather | bytes 1179648 | tf_op jit(solution)/shard_map/all_gather | solution.py:86
  153.3 3.0 %gather_fusion.2 = bf16[512,2,192]{2,1,0:T(2,128)(2,1)} fusion(bf16[2,1024,192]{2,0,1:T(2,128)(2,1)S(1)} %bitcast.101, s32[1024]{0:T(1024)S(1)} %pad_clamp_fusion), kind=kCustom, calls=%fused_computation.clone | custom fusion | bytes 788480 | tf_op jit(solution)/shard_map/jit(_take)/gather | solution.py:89
  156.3 4.2 %gather_fusion.3 = bf16[1024,2,192]{2,1,0:T(2,128)(2,1)S(1)} fusion(bf16[2,1024,192]{2,0,1:T(2,128)(2,1)S(1)} %bitcast.102, s32[1024]{0:T(1024)S(1)} %fusion.99), kind=kCustom, calls=%fused_computation.1.clone | custom fusion | bytes 1576960 | tf_op jit(solution)/shard_map/jit(_take)/gather | solution.py:95
  160.5 3.0 %gather_fusion.4 = bf16[512,2,192]{2,1,0:T(2,128)(2,1)} fusion(bf16[2,1024,192]{2,0,1:T(2,128)(2,1)S(1)} %bitcast.99, s32[1024]{0:T(1024)S(1)} %pad_clamp_fusion), kind=kCustom, calls=%fused_computation.2.clone | custom fusion | bytes 788480 | tf_op jit(solution)/shard_map/jit(_take)/gather | solution.py:89
  163.5 4.2 %gather_fusion.5 = bf16[1024,2,192]{2,1,0:T(2,128)(2,1)S(1)} fusion(bf16[2,1024,192]{2,0,1:T(2,128)(2,1)S(1)} %bitcast.100, s32[1024]{0:T(1024)S(1)} %fusion.99), kind=kCustom, calls=%fused_computation.3.clone | custom fusion | bytes 1576960 | tf_op jit(solution)/shard_map/jit(_take)/gather | solution.py:95
  167.7 1.3 copy.63
  169.0 1.3 copy.72
  170.5 4.2 %fusion.17 = (bf16[2,1024,192]{2,0,1:T(2,128)(2,1)S(1)}, bf16[2,1024,192]{2,0,1:T(2,128)(2,1)S(1)}) fusion(bf16[1024,2,192]{2,1,0:T(2,128)(2,1)S(1)} %gather_fusion.5, pred[1024]{0:T(1024)(128)(4,1)S(1)} %get-tuple-element.11, bf16[1024,2,192]{2,1,0:T(2,128)(2,1)S(1)} %gather_fusion.3), kind=kLoop, calls=%fused_computation.34 | loop fusion | flops 786432 | bytes 3146752 | tf_op jit(solution)/shard_map/jit(_take)/select_n | solution.py:95
  174.8 1.6 fusion.12
  176.3 4.0 %multiply_convert_fusion = bf16[2,1024,1024]{2,1,0:T(8,128)(2,1)} fusion(f32[2,1024,1024]{2,1,0:T(8,128)S(1)} %fusion.12, bf16[2,1024,192]{2,0,1:T(2,128)(2,1)S(1)} %get-tuple-element.32, bf16[2,512,192]{1,2,0:T(8,128)(2,1)S(1)} %bitcast.111, bf16[2,512,192]{1,2,0:T(8,128)(2,1)S(1)} %bitcast.104), kind=kOutput, calls=%fused_computation.6 | convolution fusion | flops 813170688 | bytes 14155776 | tf_op jit(solution)/shard_map/kpx,kqx->kpq/dot_general | solution.py:96
  (48 shorter events, 9.9 us)
Async XLA Ops:
  0.0 118.1 %copy-start = (s32[512]{0:T(512)S(1)}, s32[512]{0:T(512)}, u32[]{:S(2)}) copy-start(s32[512]{0:T(512)} %param.11) | copy-start | bytes 6148
  7.2 3.9 %copy-start.3 = (bf16[2,2,2,52736]{3,2,1,0:T(2,128)(2,1)S(1)}, bf16[2,2,2,52736]{3,2,1,0:T(2,128)(2,1)}, u32[]{:S(2)}) copy-start(bf16[2,2,2,52736]{3,2,1,0:T(2,128)(2,1)} %param.8) | copy-start | bytes 2531332
  17.4 1.6 copy-start.2
  17.7 1.3 copy-start.1
  28.0 48.0 %all-to-all-start = ((bf16[2,32,8,2,192]{4,2,3,0,1:T(8,128)(2,1)}), bf16[2,32,8,2,192]{4,2,3,0,1:T(8,128)(2,1)S(1)}, u32[]{:S(2)}, u32[]{:S(2)}) async-start(bf16[2,32,8,2,192]{4,2,3,0,1:T(8,128)(2,1)} %copy.57), calls=%async_computation | async-start | bytes 1048576 | tf_op jit(solution)/shard_map/all_to_all | solution.py:72
  76.0 35.7 %all-to-all-start.2 = ((bf16[2,32,8,2,192]{4,2,3,0,1:T(8,128)(2,1)}), bf16[2,32,8,2,192]{4,2,3,0,1:T(8,128)(2,1)S(1)}, u32[]{:S(2)}, u32[]{:S(2)}) async-start(bf16[2,32,8,2,192]{4,2,3,0,1:T(8,128)(2,1)} %copy.66), calls=%async_computation.2 | async-start | bytes 1048576 | tf_op jit(solution)/shard_map/all_to_all | solution.py:72
  111.7 14.9 %all-to-all-start.1 = ((bf16[2,1,8,64,192]{4,3,0,1,2:T(8,128)(2,1)}), bf16[2,1,8,64,192]{4,3,0,1,2:T(8,128)(2,1)S(1)}, u32[]{:S(2)}, u32[]{:S(2)}) async-start(bf16[2,1,8,64,192]{4,3,0,1,2:T(8,128)(2,1)} %copy.59), calls=%async_computation.1 | async-start | bytes 1048576 | tf_op jit(solution)/shard_map/all_to_all | solution.py:71
  126.6 14.5 %all-to-all-start.3 = ((bf16[2,1,8,64,192]{4,3,0,1,2:T(8,128)(2,1)}), bf16[2,1,8,64,192]{4,3,0,1,2:T(8,128)(2,1)S(1)}, u32[]{:S(2)}, u32[]{:S(2)}) async-start(bf16[2,1,8,64,192]{4,3,0,1,2:T(8,128)(2,1)} %copy.68), calls=%async_computation.3 | async-start | bytes 1048576 | tf_op jit(solution)/shard_map/all_to_all | solution.py:71
where the time goes:
time: 181 us; the launch traced here: 180 us
  waiting for transfers between devices  56.1 us (31%)
  local copies, waits for them, and re-layouts  44.3 us (24%)
  starting transfers between devices  34.6 us (19%)
  matrix products  19.4 us (11%)
  other arithmetic  15.6 us (9%)
  blocking collectives  10.1 us (6%)
    all_to_all x2, waiting for transfers between devices, shards(): lax.all_to_all(result.reshape(CAP, chan_count, cols_count, local_inputs,...  47.3 us
    all_to_all x2, starting transfers between devices, shards(): lax.all_to_all(result.reshape(CAP, chan_count, cols_count, local_inputs,...  22.3 us
    dot_general x2, matrix products, shards(): jnp.einsum('iasj,ajbkg->kgibs', summed, table, precision=lax.Precision.HI...  13.8 us
    all_to_all x2, starting transfers between devices, shards(): lax.all_to_all(lax.all_to_all(result.reshape(CAP, chan_count, cols_count,...  12.3 us
    all_gather x2, blocking collectives, shards(): gathered = lax.all_gather(turned, 'row', axis=3, tiled=True)  10.1 us
    all_to_all x2, waiting for transfers between devices, shards(): lax.all_to_all(lax.all_to_all(result.reshape(CAP, chan_count, cols_count,...  8.86 us
    gather x4, local copies, waits for them, and re-layouts, shards(): rows = jnp.take(flat, row_pick, axis=1)  8.64 us
    gather x2, local copies, waits for them, and re-layouts, shards(): columns = jnp.take(flat, located, axis=1)  8.34 us
  transfers between devices with their start and end apart: 4, of which 4 were waited for; matrix products, arithmetic and copies ran while one was open for 12% of the time, Pallas kernels for 0%

commit v1 on v0

--- a/solution.py
+++ b/solution.py
@@ -68,20 +68,28 @@
                 * signal[:, :, tap_index : tap_index + spec_len, :]
             )
         result = jnp.einsum("iasj,ajbkg->kgibs", summed, table, precision=lax.Precision.HIGHEST)
-        turned = lax.all_to_all(
+        turned = jnp.concatenate(
             lax.all_to_all(
-                result.reshape(CAP, chan_count, cols_count, local_inputs, 2 * spec_len).astype(
-                    jnp.bfloat16
+                jnp.stack(
+                    jnp.split(
+                        lax.all_to_all(
+                            result.reshape(
+                                CAP, chan_count, cols_count, local_inputs, 2 * spec_len
+                            ).astype(jnp.bfloat16),
+                            "chan",
+                            split_axis=1,
+                            concat_axis=3,
+                            tiled=True,
+                        ),
+                        lax.axis_size("col"),
+                        axis=2,
+                    )
                 ),
-                "chan",
-                split_axis=1,
-                concat_axis=3,
-                tiled=True,
+                "col",
+                0,
+                0,
             ),
-            "col",
-            split_axis=2,
-            concat_axis=3,
-            tiled=True,
+            axis=3,
         )
         gathered = lax.all_gather(turned, "row", axis=3, tiled=True)
         flat = gathered.reshape(CAP, total_inputs, -1)

time: 181 us -> 170 us (0.939)
  waiting for transfers between devices: 56.1 us -> 37.3 us
  local copies, waits for them, and re-layouts: 44.3 us -> 54.8 us
    all_to_all x2, waiting for transfers between devices: 47.3 us -> 35 us  [shards(): lax.all_to_all(result.reshape(CAP, chan_count, cols_count, local_inputs,...]
    unnamed x8 -> x22, local copies, waits for them, and re-layouts: 1.33 us -> 10.2 us
    all_to_all x2, waiting for transfers between devices: 8.86 us -> 2.34 us  [shards(): lax.all_to_all(jnp.stack(jnp.split(lax.all_to_all(result.reshape(CAP, cha...]
    split x0 -> x2, local copies, waits for them, and re-layouts: none -> 2.25 us  [shards(): jnp.split(lax.all_to_all(result.reshape(CAP, chan_count, cols_count, loca...]
    all_to_all x4 -> x2, local copies, waits for them, and re-layouts: 1.88 us -> 0.07 us  [shards(): lax.all_to_all(result.reshape(CAP, chan_count, cols_count, local_inputs,...]
  transfers between devices with their start and end apart: 4 -> 4, of which waited for: 4 -> 3; matrix products, arithmetic and copies ran while one was open for 12% -> 24% of each run, Pallas kernels for 0% -> 0%
where the time goes in v1:
time: 170 us; the launch traced here: 169 us
  local copies, waits for them, and re-layouts  54.8 us (32%)
  waiting for transfers between devices  37.3 us (22%)
  starting transfers between devices  33.1 us (19%)
  matrix products  19.2 us (11%)
  other arithmetic  15.6 us (9%)
  blocking collectives  8.96 us (5%)
    all_to_all x2, waiting for transfers between devices, shards(): lax.all_to_all(result.reshape(CAP, chan_count, cols_count, local_inputs,...  35 us
    all_to_all x2, starting transfers between devices, shards(): lax.all_to_all(result.reshape(CAP, chan_count, cols_count, local_inputs,...  22.4 us
    dot_general x2, matrix products, shards(): jnp.einsum('iasj,ajbkg->kgibs', summed, table, precision=lax.Precision.HI...  13.6 us
    all_to_all x2, starting transfers between devices, shards(): lax.all_to_all(jnp.stack(jnp.split(lax.all_to_all(result.reshape(CAP, cha...  10.7 us
    unnamed x22, local copies, waits for them, and re-layouts  10.2 us
    all_gather x2, blocking collectives, shards(): gathered = lax.all_gather(turned, 'row', axis=3, tiled=True)  8.96 us
    gather x4, local copies, waits for them, and re-layouts, shards(): rows = jnp.take(flat, row_pick, axis=1)  8.63 us
    gather x2, local copies, waits for them, and re-layouts, shards(): columns = jnp.take(flat, located, axis=1)  8.34 us
  transfers between devices with their start and end apart: 4, of which 3 were waited for; matrix products, arithmetic and copies ran while one was open for 24% of the time, Pallas kernels for 0%

profile of v1, /device:TPU:1, one launch (start us, length us, event | category | flops | bytes accessed | tf_op | source)
XLA Modules:
  0.0 169.3 jit_solution(9420044969200141294)
XLA Ops:
  3.4 3.8 %sort.17 = (s32[384]{0:T(512)}, s32[384]{0:T(512)S(1)}) sort(s32[384]{0:T(512)S(1)} %iota_add_fusion, s32[384]{0:T(512)S(1)} %iota.40), dimensions={0}, to_apply=%region_3.4 | sort | flops 3456 | bytes 6144 | tf_op jit(solution)/shard_map/jit(argsort)/sort | solution.py:16
  7.2 3.5 %gather_fusion = s32[512]{0:T(512)S(1)} fusion(s32[384]{0:T(512)S(1)} %get-tuple-element.8, s32[1024]{0:T(1024)S(1)} %pad_clamp_fusion.1), kind=kCustom, calls=%fused_computation.4 | custom fusion | bytes 6144 | tf_op jit(solution)/shard_map/jit(_take)/gather | solution.py:24
  11.7 1.5 reshape.304
  13.2 4.2 %fusion.71 = (f32[512,1,2,256]{3,0,2,1:T(8,128)S(1)}, f32[512,1,2,256]{3,0,2,1:T(8,128)S(1)}, f32[512,1,2,256]{3,0,2,1:T(8,128)S(1)}) fusion(f32[2,256]{1,0:T(2,128)S(1)} %compare_select_fusion.6, s32[2,256]{1,0:T(2,128)S(1)} %copy.220), kind=kLoop, calls=%fused_computation.100 | loop fusion | flops 4456448 | bytes 3149824 | tf_op jit(solution)/shard_map/neg | solution.py:45
  17.7 1.3 copy-done.1
  19.0 4.6 %fusion.7 = bf16[2,256,2,2,96]{1,4,2,0,3:T(8,128)(2,1)} fusion(f32[1,512,2,2,256]{4,1,0,3,2:T(8,128)S(1)} %get-tuple-element.14, f32[1,512,2,2,256]{4,1,0,3,2:T(8,128)S(1)} %get-tuple-element.13, f32[2,2,103,512]{3,2,1,0:T(8,128)S(1)} %copy-done.2, f32[512]{0:T(512)S(1)} %bitcast.163, f32[512]{0:T(512)S(1)} %bitcast.165, f32[512]{0:T(512)S(1)} %bitcast.153, ...), kind=kOutput, calls=%fused_computation.22 | convolution fusion | flops 2420113408 | bytes 10895360 | tf_op jit(solution)/shard_map/iasj,ajbkg->kgibs/dot_general | solution.py:70
  23.6 1.3 copy.230
  26.1 1.9 %copy.231 = bf16[2,32,8,2,192]{4,2,3,0,1:T(8,128)(2,1)} copy(bf16[2,32,8,2,192]{4,2,1,3,0:T(8,128)(2,1)} %convert_element_type.73) | data formatting | bytes 786432 | tf_op jit(solution)/shard_map/convert_element_type | solution.py:78
  28.0 17.0 %all-to-all-start.2 = ((bf16[2,32,8,2,192]{4,2,3,0,1:T(8,128)(2,1)}), bf16[2,32,8,2,192]{4,2,3,0,1:T(8,128)(2,1)S(1)}, u32[]{:S(2)}, u32[]{:S(2)}) async-start(bf16[2,32,8,2,192]{4,2,3,0,1:T(8,128)(2,1)} %copy.231), calls=%async_computation.2 | async-start | bytes 1048576 | tf_op jit(solution)/shard_map/all_to_all | solution.py:75
  45.0 1.5 reshape.303
  46.5 9.0 %fusion.6 = bf16[2,256,2,2,96]{1,4,2,0,3:T(8,128)(2,1)} fusion(f32[1,512,2,2,256]{4,1,0,3,2:T(8,128)} %copy-done.1, f32[1,512,2,2,256]{4,1,0,3,2:T(8,128)S(1)} %get-tuple-element.13, f32[2,2,103,512]{3,2,1,0:T(8,128)} %reshape.303, f32[512]{0:T(512)S(1)} %bitcast.164, f32[512]{0:T(512)S(1)} %bitcast.166, f32[512]{0:T(512)S(1)} %bitcast.154, ...), kind=kOutput, calls=%fused_computation.21 | convolution fusion | flops 2420113408 | bytes 10895360 | tf_op jit(solution)/shard_map/iasj,ajbkg->kgibs/dot_general | solution.py:70
  55.5 1.3 copy.222
  58.1 6.9 %gather_fusion.1 = s32[1024]{0:T(1024)S(1)} fusion(s32[512]{0:T(512)S(1)} %copy-done, s32[1024]{0:T(1024)S(1)} %broadcast_clamp_fusion), kind=kCustom, calls=%fused_computation.5 | custom fusion | bytes 12288 | tf_op jit(solution)/shard_map/jit(_take)/gather | solution.py:49
  65.1 10.8 %all-to-all-done.2 = bf16[2,32,8,2,192]{4,2,3,0,1:T(8,128)(2,1)S(1)} async-done(((bf16[2,32,8,2,192]{4,2,3,0,1:T(8,128)(2,1)}), bf16[2,32,8,2,192]{4,2,3,0,1:T(8,128)(2,1)S(1)}, u32[]{:S(2)}, u32[]{:S(2)}) %all-to-all-start.2) | async-done | bytes 393248 | tf_op jit(solution)/shard_map/all_to_all | solution.py:75
  75.9 5.3 %all-to-all-start = ((bf16[2,32,8,2,192]{4,2,3,0,1:T(8,128)(2,1)}), bf16[2,32,8,2,192]{4,2,3,0,1:T(8,128)(2,1)S(1)}, u32[]{:S(2)}, u32[]{:S(2)}) async-start(bf16[2,32,8,2,192]{4,2,3,0,1:T(8,128)(2,1)} %copy.223), calls=%async_computation | async-start | bytes 1048576 | tf_op jit(solution)/shard_map/all_to_all | solution.py:75
  81.3 1.1 fusion.105
  87.5 24.2 %all-to-all-done = bf16[2,32,8,2,192]{4,2,3,0,1:T(8,128)(2,1)S(1)} async-done(((bf16[2,32,8,2,192]{4,2,3,0,1:T(8,128)(2,1)}), bf16[2,32,8,2,192]{4,2,3,0,1:T(8,128)(2,1)S(1)}, u32[]{:S(2)}, u32[]{:S(2)}) %all-to-all-start) | async-done | bytes 393248 | tf_op jit(solution)/shard_map/all_to_all | solution.py:75
  111.7 6.4 %all-to-all-start.3 = ((bf16[8,2,1,1,64,192]{5,4,1,3,2,0:T(8,128)(2,1)}), bf16[8,2,1,1,64,192]{5,4,1,3,2,0:T(8,128)(2,1)S(1)}, u32[]{:S(2)}, u32[]{:S(2)}) async-start(bf16[8,2,1,1,64,192]{5,4,1,3,2,0:T(8,128)(2,1)} %bitcast_dynamic-update-slice_fusion), calls=%async_computation.3 | async-start | bytes 1048576 | tf_op jit(solution)/shard_map/all_to_all | solution.py:72
  118.1 1.1 fusion.106
  124.3 2.3 %all-to-all-done.3 = bf16[8,2,1,1,64,192]{5,4,1,3,2,0:T(8,128)(2,1)S(1)} async-done(((bf16[8,2,1,1,64,192]{5,4,1,3,2,0:T(8,128)(2,1)}), bf16[8,2,1,1,64,192]{5,4,1,3,2,0:T(8,128)(2,1)S(1)}, u32[]{:S(2)}, u32[]{:S(2)}) %all-to-all-start.3) | async-done | bytes 393248 | tf_op jit(solution)/shard_map/all_to_all | solution.py:72
  126.6 4.3 %all-to-all-start.1 = ((bf16[8,2,1,1,64,192]{5,4,1,3,2,0:T(8,128)(2,1)}), bf16[8,2,1,1,64,192]{5,4,1,3,2,0:T(8,128)(2,1)S(1)}, u32[]{:S(2)}, u32[]{:S(2)}) async-start(bf16[8,2,1,1,64,192]{5,4,1,3,2,0:T(8,128)(2,1)} %bitcast_dynamic-update-slice_fusion.8), calls=%async_computation.1 | async-start | bytes 1048576 | tf_op jit(solution)/shard_map/all_to_all | solution.py:72
  131.2 6.4 %all_gather.7 = bf16[2,1,1,1024,192]{3,4,2,1,0:T(8,128)(2,1)S(1)} all-gather(bf16[2,1,1,512,192]{3,4,2,1,0:T(8,128)(2,1)S(1)} %copy.234), channel_id=1, replica_groups=mesh['chan'=32,'row'=2,'col'=8] {'row'}, dimensions={3}, use_global_device_ids=true | all-gather | bytes 1179648 | tf_op jit(solution)/shard_map/all_gather | solution.py:94
  138.4 3.0 %gather_fusion.4 = bf16[512,2,192]{2,1,0:T(2,128)(2,1)} fusion(bf16[2,1024,192]{2,0,1:T(2,128)(2,1)S(1)} %bitcast.135, s32[1024]{0:T(1024)S(1)} %get-tuple-element.52), kind=kCustom, calls=%fused_computation.2.clone | custom fusion | bytes 788480 | tf_op jit(solution)/shard_map/jit(_take)/gather | solution.py:97
  141.5 4.2 %gather_fusion.5 = bf16[1024,2,192]{2,1,0:T(2,128)(2,1)S(1)} fusion(bf16[2,1024,192]{2,0,1:T(2,128)(2,1)S(1)} %bitcast.136, s32[1024]{0:T(1024)S(1)} %get-tuple-element.53), kind=kCustom, calls=%fused_computation.3.clone | custom fusion | bytes 1576960 | tf_op jit(solution)/shard_map/jit(_take)/gather | solution.py:103
  145.9 2.6 %all_gather.6 = bf16[2,1,1,1024,192]{3,4,2,1,0:T(8,128)(2,1)S(1)} all-gather(bf16[2,1,1,512,192]{3,4,2,1,0:T(8,128)(2,1)S(1)} %copy.226), channel_id=1, replica_groups=mesh['chan'=32,'row'=2,'col'=8] {'row'}, dimensions={3}, use_global_device_ids=true | all-gather | bytes 1179648 | tf_op jit(solution)/shard_map/all_gather | solution.py:94
  149.4 3.0 %gather_fusion.2 = bf16[512,2,192]{2,1,0:T(2,128)(2,1)} fusion(bf16[2,1024,192]{2,0,1:T(2,128)(2,1)S(1)} %bitcast.133, s32[1024]{0:T(1024)S(1)} %get-tuple-element.52), kind=kCustom, calls=%fused_computation.clone | custom fusion | bytes 788480 | tf_op jit(solution)/shard_map/jit(_take)/gather | solution.py:97
  152.4 4.2 %gather_fusion.3 = bf16[1024,2,192]{2,1,0:T(2,128)(2,1)S(1)} fusion(bf16[2,1024,192]{2,0,1:T(2,128)(2,1)S(1)} %bitcast.134, s32[1024]{0:T(1024)S(1)} %get-tuple-element.53), kind=kCustom, calls=%fused_computation.1.clone | custom fusion | bytes 1576960 | tf_op jit(solution)/shard_map/jit(_take)/gather | solution.py:103
  156.6 1.3 copy.236
  157.9 1.3 copy.228
  159.4 4.2 %fusion.17 = (bf16[2,1024,192]{2,0,1:T(2,128)(2,1)S(1)}, bf16[2,1024,192]{2,0,1:T(2,128)(2,1)S(1)}) fusion(bf16[1024,2,192]{2,1,0:T(2,128)(2,1)S(1)} %gather_fusion.5, pred[1024]{0:T(1024)(128)(4,1)S(1)} %get-tuple-element.11, bf16[1024,2,192]{2,1,0:T(2,128)(2,1)S(1)} %gather_fusion.3), kind=kLoop, calls=%fused_computation.34 | loop fusion | flops 786432 | bytes 3146752 | tf_op jit(solution)/shard_map/jit(_take)/select_n | solution.py:103
  163.7 1.6 fusion.12
  165.2 4.0 %multiply_convert_fusion = bf16[2,1024,1024]{2,1,0:T(8,128)(2,1)} fusion(f32[2,1024,1024]{2,1,0:T(8,128)S(1)} %fusion.12, bf16[2,1024,192]{2,0,1:T(2,128)(2,1)S(1)} %get-tuple-element.48, bf16[2,512,192]{1,2,0:T(8,128)(2,1)S(1)} %bitcast.147, bf16[2,512,192]{1,2,0:T(8,128)(2,1)S(1)} %bitcast.140), kind=kOutput, calls=%fused_computation.6 | convolution fusion | flops 813170688 | bytes 14155776 | tf_op jit(solution)/shard_map/kpx,kqx->kpq/dot_general | solution.py:104
  (63 shorter events, 19.7 us)
Async XLA Ops:
  0.0 58.1 %copy-start = (s32[512]{0:T(512)S(1)}, s32[512]{0:T(512)}, u32[]{:S(2)}) copy-start(s32[512]{0:T(512)} %param.11) | copy-start | bytes 6148
  7.2 3.9 %copy-start.3 = (bf16[2,2,2,52736]{3,2,1,0:T(2,128)(2,1)S(1)}, bf16[2,2,2,52736]{3,2,1,0:T(2,128)(2,1)}, u32[]{:S(2)}) copy-start(bf16[2,2,2,52736]{3,2,1,0:T(2,128)(2,1)} %param.8) | copy-start | bytes 2531332
  17.4 1.6 copy-start.2
  17.7 1.3 copy-start.1
  28.0 47.9 %all-to-all-start.2 = ((bf16[2,32,8,2,192]{4,2,3,0,1:T(8,128)(2,1)}), bf16[2,32,8,2,192]{4,2,3,0,1:T(8,128)(2,1)S(1)}, u32[]{:S(2)}, u32[]{:S(2)}) async-start(bf16[2,32,8,2,192]{4,2,3,0,1:T(8,128)(2,1)} %copy.231), calls=%async_computation.2 | async-start | bytes 1048576 | tf_op jit(solution)/shard_map/all_to_all | solution.py:75
  75.9 35.8 %all-to-all-start = ((bf16[2,32,8,2,192]{4,2,3,0,1:T(8,128)(2,1)}), bf16[2,32,8,2,192]{4,2,3,0,1:T(8,128)(2,1)S(1)}, u32[]{:S(2)}, u32[]{:S(2)}) async-start(bf16[2,32,8,2,192]{4,2,3,0,1:T(8,128)(2,1)} %copy.223), calls=%async_computation | async-start | bytes 1048576 | tf_op jit(solution)/shard_map/all_to_all | solution.py:75
  111.7 14.9 %all-to-all-start.3 = ((bf16[8,2,1,1,64,192]{5,4,1,3,2,0:T(8,128)(2,1)}), bf16[8,2,1,1,64,192]{5,4,1,3,2,0:T(8,128)(2,1)S(1)}, u32[]{:S(2)}, u32[]{:S(2)}) async-start(bf16[8,2,1,1,64,192]{5,4,1,3,2,0:T(8,128)(2,1)} %bitcast_dynamic-update-slice_fusion), calls=%async_computation.3 | async-start | bytes 1048576 | tf_op jit(solution)/shard_map/all_to_all | solution.py:72
  126.6 19.0 %all-to-all-start.1 = ((bf16[8,2,1,1,64,192]{5,4,1,3,2,0:T(8,128)(2,1)}), bf16[8,2,1,1,64,192]{5,4,1,3,2,0:T(8,128)(2,1)S(1)}, u32[]{:S(2)}, u32[]{:S(2)}) async-start(bf16[8,2,1,1,64,192]{5,4,1,3,2,0:T(8,128)(2,1)} %bitcast_dynamic-update-slice_fusion.8), calls=%async_computation.1 | async-start | bytes 1048576 | tf_op jit(solution)/shard_map/all_to_all | solution.py:72
